TPU v7x, 32 devices: a whole 2x2x4 slice. The times are simulated.
32 devices in a mesh: date: 4 (over y, core), space: 8 (over z, x).
Axes of the slice: x: 2, y: 2, z: 4, core: 2. Of those that a mesh axis runs over, the one named last changes fastest.
Arguments:
- stack: float32 [2, 28, 64, 1024], P(None, 'date', 'space'), may hold values from -6 to 6
Outputs:
- coherence: float32 [14, 28, 64, 1024], P(None, None, 'space', 'date')
All inputs are finite; a program needn't handle non-finite values.
Results may differ from a plain program's by a relative error of at most 0.000068.
Values sent between devices are 32-bit elements; how exact they have to be, the bound alone decides.
A program may use at most 64 MiB of HBM per device.

v0:
```python
import jax
import jax.numpy as jnp
from jax import lax
from jax.sharding import PartitionSpec as P

WIN_AZ = 11
WIN_RG = 23


def padded(shard, sides, width):
    for axis, dim in sides:
        peers, length = (lax.axis_size(axis), shard.shape[dim])
        up = [(i, (i + 1) % peers) for i in range(peers - 1)]
        down = [(j, i) for i, j in up]
        last = lax.slice_in_dim(shard, length - width, length, axis=dim)
        initial = lax.slice_in_dim(shard, 0, width, axis=dim)
        before = lax.ppermute(last, axis, up)
        after = lax.ppermute(initial, axis, down)
        shard = jnp.concatenate([before, shard, after], axis=dim)
    return shard


def band_tables(rows, cols):
    span_az = WIN_AZ - 1
    span_rg = WIN_RG - 1
    out_rows = lax.broadcasted_iota(jnp.int32, (rows, rows + span_az), 0)
    in_rows = lax.broadcasted_iota(jnp.int32, (rows, rows + span_az), 1)
    band_az = jnp.where((in_rows >= out_rows) & (in_rows <= out_rows + span_az), 1.0, 0.0).astype(
        jnp.float32
    )
    in_cols = lax.broadcasted_iota(jnp.int32, (cols + span_rg, cols), 0)
    out_cols = lax.broadcasted_iota(jnp.int32, (cols + span_rg, cols), 1)
    band_rg = jnp.where((in_cols >= out_cols) & (in_cols <= out_cols + span_rg), 1.0, 0.0).astype(
        jnp.float32
    )
    return (band_az, band_rg)


def boxcar_local(values, band_az, band_rg):
    along_range = jnp.einsum(
        "dac,cb->dab",
        values,
        band_rg,
        precision=lax.Precision.HIGHEST,
        preferred_element_type=jnp.float32,
    )
    return jnp.einsum(
        "ra,dab->drb",
        band_az,
        along_range,
        precision=lax.Precision.HIGHEST,
        preferred_element_type=jnp.float32,
    )


def body(stack):
    half_az = WIN_AZ // 2
    half_rg = WIN_RG // 2
    relaid = lax.all_to_all(stack, "date", split_axis=3, concat_axis=1, tiled=True)
    taller = padded(relaid, (("space", 2),), half_az)
    extended = padded(taller, (("date", 3),), half_rg)
    rows = extended.shape[2] - 2 * half_az
    cols = extended.shape[3] - 2 * half_rg
    dates = extended.shape[1]
    band_az, band_rg = band_tables(rows, cols)
    real_part = extended[0]
    imag_part = extended[1]
    power = boxcar_local(real_part * real_part + imag_part * imag_part, band_az, band_rg)
    doubled = jnp.concatenate([extended, extended], axis=1)
    power_doubled = jnp.concatenate([power, power], axis=0)

    def one_lag(lag):
        shift = lag + 1
        other = lax.dynamic_slice_in_dim(doubled, shift, dates, 1)
        power_other = lax.dynamic_slice_in_dim(power_doubled, shift, dates, 0)
        real_other = other[0]
        imag_other = other[1]
        cross_re = boxcar_local(real_part * real_other + imag_part * imag_other, band_az, band_rg)
        cross_im = boxcar_local(imag_part * real_other - real_part * imag_other, band_az, band_rg)
        return jnp.sqrt(cross_re * cross_re + cross_im * cross_im) / jnp.sqrt(power * power_other)

    return lax.map(one_lag, jnp.arange(dates // 2, dtype=jnp.int32))


def solution(mesh):
    in_specs = (P(None, "date", "space", None),)
    out_specs = P(None, None, "space", "date")
    return jax.shard_map(body, mesh=mesh, in_specs=in_specs, out_specs=out_specs, check_vma=False)
```

profile of v0, /device:TPU:25, one launch (start us, length us, event | category | flops | bytes accessed | tf_op | source)
XLA Modules:
  0.0 218.5 jit_solution(2523200794362016026)
XLA Ops:
  0.0 6.8 %copy.33 = f32[2,7,8,1024]{2,1,0,3:T(8,128)} copy(f32[2,7,8,1024]{3,2,1,0:T(8,128)} %param.3) | data formatting | bytes 917504 | tf_op args[0]
  6.8 5.5 %reshape.8 = f32[4,1,28672]{2,1,0:T(1,128)S(1)} reshape(f32[1024,2,7,8]{3,2,1,0:T(8,128)} %bitcast.101) | data formatting | bytes 917504
  12.3 10.7 %all_to_all.18 = f32[4,1,28672]{2,1,0:T(1,128)S(1)} all-to-all(f32[4,1,28672]{2,1,0:T(1,128)S(1)} %reshape.8), channel_id=1, replica_groups=mesh['date'=4,'space'=8] {'date'}, dimensions={0} | all-to-all | bytes 917504 | tf_op jit(solution)/shard_map/all_to_all | solution.py:59
  25.4 7.1 %reshape.9 = f32[1024,2,7,8]{3,2,1,0:T(8,128)} reshape(f32[4,28672]{1,0:T(4,128)S(1)} %reduce) | data formatting | bytes 917504
  32.5 5.1 %copy.49 = f32[2,7,8,4,256]{4,3,2,1,0:T(4,128)S(1)} copy(f32[2,7,8,4,256]{2,1,0,4,3:T(8,128)} %bitcast.100) | data formatting | bytes 917504 | tf_op jit(solution)/shard_map/all_to_all | solution.py:59
  37.9 3.1 %collective-permute-start = (f32[2,28,5,256]{3,1,2,0:T(8,128)S(1)}, f32[2,28,5,256]{3,1,2,0:T(8,128)S(1)}, u32[]{:S(2)}, u32[]{:S(2)}) collective-permute-start(f32[2,28,5,256]{3,1,2,0:T(8,128)S(1)} %copy.78), channel_id=1, source_target_pairs={{0,1},{1,2},{2,3},{3,4},{4,5},{5,6},{6,7},{8,9},{9,10},{10,11},{11... | collective-permute-start | bytes 860168 | tf_op jit(solution)/shard_map/ppermute | solution.py:17
  41.1 3.1 %collective-permute-start.1 = (f32[2,28,5,256]{3,1,2,0:T(8,128)S(1)}, f32[2,28,5,256]{3,1,2,0:T(8,128)S(1)}, u32[]{:S(2)}, u32[]{:S(2)}) collective-permute-start(f32[2,28,5,256]{3,1,2,0:T(8,128)S(1)} %copy.79), channel_id=1, source_target_pairs={{1,0},{2,1},{3,2},{4,3},{5,4},{6,5},{7,6},{9,8},{10,9},{11,10},{12... | collective-permute-start | bytes 860168 | tf_op jit(solution)/shard_map/ppermute | solution.py:18
  44.2 5.0 %collective-permute-done = f32[2,28,5,256]{3,1,2,0:T(8,128)S(1)} collective-permute-done((f32[2,28,5,256]{3,1,2,0:T(8,128)S(1)}, f32[2,28,5,256]{3,1,2,0:T(8,128)S(1)}, u32[]{:S(2)}, u32[]{:S(2)}) %collective-permute-start) | collective-permute-done | bytes 286752 | tf_op jit(solution)/shard_map/ppermute | solution.py:17
  49.4 7.9 %collective-permute-done.1 = f32[2,28,5,256]{3,1,2,0:T(8,128)S(1)} collective-permute-done((f32[2,28,5,256]{3,1,2,0:T(8,128)S(1)}, f32[2,28,5,256]{3,1,2,0:T(8,128)S(1)}, u32[]{:S(2)}, u32[]{:S(2)}) %collective-permute-start.1) | collective-permute-done | bytes 286752 | tf_op jit(solution)/shard_map/ppermute | solution.py:18
  63.2 4.4 %collective-permute-done.3 = f32[2,28,18,11]{1,0,3,2:T(2,128)S(1)} collective-permute-done((f32[2,28,18,11]{1,0,3,2:T(2,128)S(1)}, f32[2,28,18,11]{1,0,3,2:T(2,128)S(1)}, u32[]{:S(2)}, u32[]{:S(2)}) %collective-permute-start.3) | collective-permute-done | bytes 44384 | tf_op jit(solution)/shard_map/ppermute | solution.py:18
  68.9 3.0 %maximum_maximum_fusion = f32[2,56,18,278]{3,1,2,0:T(8,128)} fusion(f32[2,28,18,11]{3,1,2,0:T(8,128)S(1)} %copy.42, f32[2,28,18,256]{3,1,2,0:T(8,128)S(1)} %constant_dynamic-update-slice_fusion, f32[2,28,18,11]{3,1,2,0:T(8,128)S(1)} %copy.41), kind=kLoop, calls=%fused_computation.56 | loop fusion | flops 2802240 | bytes 3362688 | tf_op jit(solution)/shard_map/concatenate | solution.py:69
  75.0 143.4 %while.14 = (s32[]{:T(128)}, f32[14,28,8,256]{3,2,1,0:T(8,128)}, s32[14]{0:T(128)S(1)}, f32[2,56,18,278]{3,1,2,0:T(8,128)}, f32[28,18,278]{2,1,0:T(8,128)S(1)}, ...) while((s32[]{:T(128)}, f32[14,28,8,256]{3,2,1,0:T(8,128)}, ...), condition=%wide.region_1.2_spmd.clone.clone, body=%wide.region_0.1_spmd.clone.clone.sunk | while | flops 887318656 | bytes 9939487 | solution.py:82
  78.9 2.3 %fusion.101 = f32[28,18,256]{2,1,0:T(8,128)S(1)} fusion(f32[28,18,278]{2,1,0:T(8,128)S(1)} %get-tuple-element.357, f32[1,28,18,278]{3,1,2,0:T(8,128)S(1)} %get-tuple-element.320, f32[28,18,278]{2,1,0:T(8,128)S(1)} %get-tuple-element.356, f32[1,28,18,278]{3,1,2,0:T(8,128)S(1)} %get-tuple-element.321, s32[256]{0:T(256)S(1)} %get-tuple-element.360), kind=kOutput, calls=%fused_computation.14.clone.1 | convolution fusion | flops 431129088 | bytes 2758912 | tf_op jit(solution)/shard_map/while/body/eval_jaxpr/dac,cb->dab/dot_general | solution.py:40
  89.1 2.3 %fusion.101 = f32[28,18,256]{2,1,0:T(8,128)S(1)} fusion(f32[28,18,278]{2,1,0:T(8,128)S(1)} %get-tuple-element.357, f32[1,28,18,278]{3,1,2,0:T(8,128)S(1)} %get-tuple-element.320, f32[28,18,278]{2,1,0:T(8,128)S(1)} %get-tuple-element.356, f32[1,28,18,278]{3,1,2,0:T(8,128)S(1)} %get-tuple-element.321, s32[256]{0:T(256)S(1)} %get-tuple-element.360), kind=kOutput, calls=%fused_computation.14.clone.1 | convolution fusion | flops 431129088 | bytes 2758912 | tf_op jit(solution)/shard_map/while/body/eval_jaxpr/dac,cb->dab/dot_general | solution.py:40
  91.4 2.3 %fusion.100 = f32[28,18,256]{2,1,0:T(8,128)S(1)} fusion(f32[28,18,278]{2,1,0:T(8,128)S(1)} %get-tuple-element.356, f32[1,28,18,278]{3,1,2,0:T(8,128)S(1)} %get-tuple-element.320, f32[28,18,278]{2,1,0:T(8,128)S(1)} %get-tuple-element.357, f32[1,28,18,278]{3,1,2,0:T(8,128)S(1)} %get-tuple-element.321, s32[256]{0:T(256)S(1)} %get-tuple-element.360), kind=kOutput, calls=%fused_computation.16.clone.1 | convolution fusion | flops 431129088 | bytes 2758912 | tf_op jit(solution)/shard_map/while/body/eval_jaxpr/dac,cb->dab/dot_general | solution.py:40
  99.4 2.3 %fusion.101 = f32[28,18,256]{2,1,0:T(8,128)S(1)} fusion(f32[28,18,278]{2,1,0:T(8,128)S(1)} %get-tuple-element.357, f32[1,28,18,278]{3,1,2,0:T(8,128)S(1)} %get-tuple-element.320, f32[28,18,278]{2,1,0:T(8,128)S(1)} %get-tuple-element.356, f32[1,28,18,278]{3,1,2,0:T(8,128)S(1)} %get-tuple-element.321, s32[256]{0:T(256)S(1)} %get-tuple-element.360), kind=kOutput, calls=%fused_computation.14.clone.1 | convolution fusion | flops 431129088 | bytes 2758912 | tf_op jit(solution)/shard_map/while/body/eval_jaxpr/dac,cb->dab/dot_general | solution.py:40
  101.6 2.3 %fusion.100 = f32[28,18,256]{2,1,0:T(8,128)S(1)} fusion(f32[28,18,278]{2,1,0:T(8,128)S(1)} %get-tuple-element.356, f32[1,28,18,278]{3,1,2,0:T(8,128)S(1)} %get-tuple-element.320, f32[28,18,278]{2,1,0:T(8,128)S(1)} %get-tuple-element.357, f32[1,28,18,278]{3,1,2,0:T(8,128)S(1)} %get-tuple-element.321, s32[256]{0:T(256)S(1)} %get-tuple-element.360), kind=kOutput, calls=%fused_computation.16.clone.1 | convolution fusion | flops 431129088 | bytes 2758912 | tf_op jit(solution)/shard_map/while/body/eval_jaxpr/dac,cb->dab/dot_general | solution.py:40
  109.6 2.3 %fusion.101 = f32[28,18,256]{2,1,0:T(8,128)S(1)} fusion(f32[28,18,278]{2,1,0:T(8,128)S(1)} %get-tuple-element.357, f32[1,28,18,278]{3,1,2,0:T(8,128)S(1)} %get-tuple-element.320, f32[28,18,278]{2,1,0:T(8,128)S(1)} %get-tuple-element.356, f32[1,28,18,278]{3,1,2,0:T(8,128)S(1)} %get-tuple-element.321, s32[256]{0:T(256)S(1)} %get-tuple-element.360), kind=kOutput, calls=%fused_computation.14.clone.1 | convolution fusion | flops 431129088 | bytes 2758912 | tf_op jit(solution)/shard_map/while/body/eval_jaxpr/dac,cb->dab/dot_general | solution.py:40
  111.9 2.3 %fusion.100 = f32[28,18,256]{2,1,0:T(8,128)S(1)} fusion(f32[28,18,278]{2,1,0:T(8,128)S(1)} %get-tuple-element.356, f32[1,28,18,278]{3,1,2,0:T(8,128)S(1)} %get-tuple-element.320, f32[28,18,278]{2,1,0:T(8,128)S(1)} %get-tuple-element.357, f32[1,28,18,278]{3,1,2,0:T(8,128)S(1)} %get-tuple-element.321, s32[256]{0:T(256)S(1)} %get-tuple-element.360), kind=kOutput, calls=%fused_computation.16.clone.1 | convolution fusion | flops 431129088 | bytes 2758912 | tf_op jit(solution)/shard_map/while/body/eval_jaxpr/dac,cb->dab/dot_general | solution.py:40
  119.9 2.3 %fusion.101 = f32[28,18,256]{2,1,0:T(8,128)S(1)} fusion(f32[28,18,278]{2,1,0:T(8,128)S(1)} %get-tuple-element.357, f32[1,28,18,278]{3,1,2,0:T(8,128)S(1)} %get-tuple-element.320, f32[28,18,278]{2,1,0:T(8,128)S(1)} %get-tuple-element.356, f32[1,28,18,278]{3,1,2,0:T(8,128)S(1)} %get-tuple-element.321, s32[256]{0:T(256)S(1)} %get-tuple-element.360), kind=kOutput, calls=%fused_computation.14.clone.1 | convolution fusion | flops 431129088 | bytes 2758912 | tf_op jit(solution)/shard_map/while/body/eval_jaxpr/dac,cb->dab/dot_general | solution.py:40
  122.1 2.3 %fusion.100 = f32[28,18,256]{2,1,0:T(8,128)S(1)} fusion(f32[28,18,278]{2,1,0:T(8,128)S(1)} %get-tuple-element.356, f32[1,28,18,278]{3,1,2,0:T(8,128)S(1)} %get-tuple-element.320, f32[28,18,278]{2,1,0:T(8,128)S(1)} %get-tuple-element.357, f32[1,28,18,278]{3,1,2,0:T(8,128)S(1)} %get-tuple-element.321, s32[256]{0:T(256)S(1)} %get-tuple-element.360), kind=kOutput, calls=%fused_computation.16.clone.1 | convolution fusion | flops 431129088 | bytes 2758912 | tf_op jit(solution)/shard_map/while/body/eval_jaxpr/dac,cb->dab/dot_general | solution.py:40
  130.1 2.3 %fusion.101 = f32[28,18,256]{2,1,0:T(8,128)S(1)} fusion(f32[28,18,278]{2,1,0:T(8,128)S(1)} %get-tuple-element.357, f32[1,28,18,278]{3,1,2,0:T(8,128)S(1)} %get-tuple-element.320, f32[28,18,278]{2,1,0:T(8,128)S(1)} %get-tuple-element.356, f32[1,28,18,278]{3,1,2,0:T(8,128)S(1)} %get-tuple-element.321, s32[256]{0:T(256)S(1)} %get-tuple-element.360), kind=kOutput, calls=%fused_computation.14.clone.1 | convolution fusion | flops 431129088 | bytes 2758912 | tf_op jit(solution)/shard_map/while/body/eval_jaxpr/dac,cb->dab/dot_general | solution.py:40
  132.4 2.3 %fusion.100 = f32[28,18,256]{2,1,0:T(8,128)S(1)} fusion(f32[28,18,278]{2,1,0:T(8,128)S(1)} %get-tuple-element.356, f32[1,28,18,278]{3,1,2,0:T(8,128)S(1)} %get-tuple-element.320, f32[28,18,278]{2,1,0:T(8,128)S(1)} %get-tuple-element.357, f32[1,28,18,278]{3,1,2,0:T(8,128)S(1)} %get-tuple-element.321, s32[256]{0:T(256)S(1)} %get-tuple-element.360), kind=kOutput, calls=%fused_computation.16.clone.1 | convolution fusion | flops 431129088 | bytes 2758912 | tf_op jit(solution)/shard_map/while/body/eval_jaxpr/dac,cb->dab/dot_general | solution.py:40
  140.3 2.3 %fusion.101 = f32[28,18,256]{2,1,0:T(8,128)S(1)} fusion(f32[28,18,278]{2,1,0:T(8,128)S(1)} %get-tuple-element.357, f32[1,28,18,278]{3,1,2,0:T(8,128)S(1)} %get-tuple-element.320, f32[28,18,278]{2,1,0:T(8,128)S(1)} %get-tuple-element.356, f32[1,28,18,278]{3,1,2,0:T(8,128)S(1)} %get-tuple-element.321, s32[256]{0:T(256)S(1)} %get-tuple-element.360), kind=kOutput, calls=%fused_computation.14.clone.1 | convolution fusion | flops 431129088 | bytes 2758912 | tf_op jit(solution)/shard_map/while/body/eval_jaxpr/dac,cb->dab/dot_general | solution.py:40
  142.6 2.3 %fusion.100 = f32[28,18,256]{2,1,0:T(8,128)S(1)} fusion(f32[28,18,278]{2,1,0:T(8,128)S(1)} %get-tuple-element.356, f32[1,28,18,278]{3,1,2,0:T(8,128)S(1)} %get-tuple-element.320, f32[28,18,278]{2,1,0:T(8,128)S(1)} %get-tuple-element.357, f32[1,28,18,278]{3,1,2,0:T(8,128)S(1)} %get-tuple-element.321, s32[256]{0:T(256)S(1)} %get-tuple-element.360), kind=kOutput, calls=%fused_computation.16.clone.1 | convolution fusion | flops 431129088 | bytes 2758912 | tf_op jit(solution)/shard_map/while/body/eval_jaxpr/dac,cb->dab/dot_general | solution.py:40
  150.6 2.3 %fusion.101 = f32[28,18,256]{2,1,0:T(8,128)S(1)} fusion(f32[28,18,278]{2,1,0:T(8,128)S(1)} %get-tuple-element.357, f32[1,28,18,278]{3,1,2,0:T(8,128)S(1)} %get-tuple-element.320, f32[28,18,278]{2,1,0:T(8,128)S(1)} %get-tuple-element.356, f32[1,28,18,278]{3,1,2,0:T(8,128)S(1)} %get-tuple-element.321, s32[256]{0:T(256)S(1)} %get-tuple-element.360), kind=kOutput, calls=%fused_computation.14.clone.1 | convolution fusion | flops 431129088 | bytes 2758912 | tf_op jit(solution)/shard_map/while/body/eval_jaxpr/dac,cb->dab/dot_general | solution.py:40
  160.8 2.3 %fusion.101 = f32[28,18,256]{2,1,0:T(8,128)S(1)} fusion(f32[28,18,278]{2,1,0:T(8,128)S(1)} %get-tuple-element.357, f32[1,28,18,278]{3,1,2,0:T(8,128)S(1)} %get-tuple-element.320, f32[28,18,278]{2,1,0:T(8,128)S(1)} %get-tuple-element.356, f32[1,28,18,278]{3,1,2,0:T(8,128)S(1)} %get-tuple-element.321, s32[256]{0:T(256)S(1)} %get-tuple-element.360), kind=kOutput, calls=%fused_computation.14.clone.1 | convolution fusion | flops 431129088 | bytes 2758912 | tf_op jit(solution)/shard_map/while/body/eval_jaxpr/dac,cb->dab/dot_general | solution.py:40
  171.1 2.3 %fusion.101 = f32[28,18,256]{2,1,0:T(8,128)S(1)} fusion(f32[28,18,278]{2,1,0:T(8,128)S(1)} %get-tuple-element.357, f32[1,28,18,278]{3,1,2,0:T(8,128)S(1)} %get-tuple-element.320, f32[28,18,278]{2,1,0:T(8,128)S(1)} %get-tuple-element.356, f32[1,28,18,278]{3,1,2,0:T(8,128)S(1)} %get-tuple-element.321, s32[256]{0:T(256)S(1)} %get-tuple-element.360), kind=kOutput, calls=%fused_computation.14.clone.1 | convolution fusion | flops 431129088 | bytes 2758912 | tf_op jit(solution)/shard_map/while/body/eval_jaxpr/dac,cb->dab/dot_general | solution.py:40
  181.3 2.3 %fusion.101 = f32[28,18,256]{2,1,0:T(8,128)S(1)} fusion(f32[28,18,278]{2,1,0:T(8,128)S(1)} %get-tuple-element.357, f32[1,28,18,278]{3,1,2,0:T(8,128)S(1)} %get-tuple-element.320, f32[28,18,278]{2,1,0:T(8,128)S(1)} %get-tuple-element.356, f32[1,28,18,278]{3,1,2,0:T(8,128)S(1)} %get-tuple-element.321, s32[256]{0:T(256)S(1)} %get-tuple-element.360), kind=kOutput, calls=%fused_computation.14.clone.1 | convolution fusion | flops 431129088 | bytes 2758912 | tf_op jit(solution)/shard_map/while/body/eval_jaxpr/dac,cb->dab/dot_general | solution.py:40
  191.6 2.3 %fusion.101 = f32[28,18,256]{2,1,0:T(8,128)S(1)} fusion(f32[28,18,278]{2,1,0:T(8,128)S(1)} %get-tuple-element.357, f32[1,28,18,278]{3,1,2,0:T(8,128)S(1)} %get-tuple-element.320, f32[28,18,278]{2,1,0:T(8,128)S(1)} %get-tuple-element.356, f32[1,28,18,278]{3,1,2,0:T(8,128)S(1)} %get-tuple-element.321, s32[256]{0:T(256)S(1)} %get-tuple-element.360), kind=kOutput, calls=%fused_computation.14.clone.1 | convolution fusion | flops 431129088 | bytes 2758912 | tf_op jit(solution)/shard_map/while/body/eval_jaxpr/dac,cb->dab/dot_general | solution.py:40
  201.8 2.3 %fusion.101 = f32[28,18,256]{2,1,0:T(8,128)S(1)} fusion(f32[28,18,278]{2,1,0:T(8,128)S(1)} %get-tuple-element.357, f32[1,28,18,278]{3,1,2,0:T(8,128)S(1)} %get-tuple-element.320, f32[28,18,278]{2,1,0:T(8,128)S(1)} %get-tuple-element.356, f32[1,28,18,278]{3,1,2,0:T(8,128)S(1)} %get-tuple-element.321, s32[256]{0:T(256)S(1)} %get-tuple-element.360), kind=kOutput, calls=%fused_computation.14.clone.1 | convolution fusion | flops 431129088 | bytes 2758912 | tf_op jit(solution)/shard_map/while/body/eval_jaxpr/dac,cb->dab/dot_general | solution.py:40
  212.1 2.3 %fusion.101 = f32[28,18,256]{2,1,0:T(8,128)S(1)} fusion(f32[28,18,278]{2,1,0:T(8,128)S(1)} %get-tuple-element.357, f32[1,28,18,278]{3,1,2,0:T(8,128)S(1)} %get-tuple-element.320, f32[28,18,278]{2,1,0:T(8,128)S(1)} %get-tuple-element.356, f32[1,28,18,278]{3,1,2,0:T(8,128)S(1)} %get-tuple-element.321, s32[256]{0:T(256)S(1)} %get-tuple-element.360), kind=kOutput, calls=%fused_computation.14.clone.1 | convolution fusion | flops 431129088 | bytes 2758912 | tf_op jit(solution)/shard_map/while/body/eval_jaxpr/dac,cb->dab/dot_general | solution.py:40
  (93 shorter events, 91.8 us)
Async XLA Ops:
  37.9 11.3 %collective-permute-start = (f32[2,28,5,256]{3,1,2,0:T(8,128)S(1)}, f32[2,28,5,256]{3,1,2,0:T(8,128)S(1)}, u32[]{:S(2)}, u32[]{:S(2)}) collective-permute-start(f32[2,28,5,256]{3,1,2,0:T(8,128)S(1)} %copy.78), channel_id=1, source_target_pairs={{0,1},{1,2},{2,3},{3,4},{4,5},{5,6},{6,7},{8,9},{9,10},{10,11},{11... | collective-permute-start | bytes 860168 | tf_op jit(solution)/shard_map/ppermute | solution.py:17
  41.1 16.2 %collective-permute-start.1 = (f32[2,28,5,256]{3,1,2,0:T(8,128)S(1)}, f32[2,28,5,256]{3,1,2,0:T(8,128)S(1)}, u32[]{:S(2)}, u32[]{:S(2)}) collective-permute-start(f32[2,28,5,256]{3,1,2,0:T(8,128)S(1)} %copy.79), channel_id=1, source_target_pairs={{1,0},{2,1},{3,2},{4,3},{5,4},{6,5},{7,6},{9,8},{10,9},{11,10},{12... | collective-permute-start | bytes 860168 | tf_op jit(solution)/shard_map/ppermute | solution.py:18
  57.9 4.9 %collective-permute-start.2 = (f32[2,28,18,11]{1,0,3,2:T(2,128)S(1)}, f32[2,28,18,11]{1,0,3,2:T(2,128)S(1)}, u32[]{:S(2)}, u32[]{:S(2)}) collective-permute-start(f32[2,28,18,11]{1,0,3,2:T(2,128)S(1)} %copy.39), channel_id=1, source_target_pairs={{0,8},{8,16},{16,24},{1,9},{9,17},{17,25},{2,10},{10,18},{18,26},{... | collective-permute-start | bytes 133064 | tf_op jit(solution)/shard_map/ppermute | solution.py:17
  60.5 7.0 %collective-permute-start.3 = (f32[2,28,18,11]{1,0,3,2:T(2,128)S(1)}, f32[2,28,18,11]{1,0,3,2:T(2,128)S(1)}, u32[]{:S(2)}, u32[]{:S(2)}) collective-permute-start(f32[2,28,18,11]{1,0,3,2:T(2,128)S(1)} %copy.40), channel_id=1, source_target_pairs={{8,0},{16,8},{24,16},{9,1},{17,9},{25,17},{10,2},{18,10},{26,18},{... | collective-permute-start | bytes 133064 | tf_op jit(solution)/shard_map/ppermute | solution.py:18
where the time goes:
time: 219 us; the launch traced here: 218 us
  matrix products  91.4 us (42%)
  local copies, waits for them, and re-layouts  63 us (29%)
  loops' own time  19.5 us (9%)
  waiting for transfers between devices  17.4 us (8%)
  blocking collectives  10.7 us (5%)
  starting transfers between devices  10.7 us (5%)
  other arithmetic  5.76 us (3%)
    dot_general x29, matrix products, boxcar_local(): jnp.einsum('dac,cb->dab', values, band_rg, precision=lax.Precision.HIGHES...  65.2 us
    dot_general x29, matrix products, boxcar_local(): jnp.einsum('ra,dab->drb', band_az, along_range, precision=lax.Precision.H...  26.2 us
    slice x14, local copies, waits for them, and re-layouts, one_lag(): real_other = other[0]  25.6 us
    unnamed x9, local copies, waits for them, and re-layouts  20.7 us
    another operation x1, loops' own time, body(): return lax.map(one_lag, jnp.arange(dates // 2, dtype=jnp.int32))  19.5 us
    ppermute x2, waiting for transfers between devices, padded(): after = lax.ppermute(initial, axis, down)  12.3 us
    all_to_all x1, blocking collectives, body(): lax.all_to_all(stack, 'date', split_axis=3, concat_axis=1, tiled=True)  10.7 us
    dynamic_slice x14, local copies, waits for them, and re-layouts, body(): return lax.map(one_lag, jnp.arange(dates // 2, dtype=jnp.int32))  9.16 us
  transfers between devices with their start and end apart: 4, of which 3 were waited for; matrix products, arithmetic and copies ran while one was open for 0% of the time, Pallas kernels for 0%

commit v1 on v0

v1 whole, which is shorter than its diff:
```python
import functools

import jax
import jax.numpy as jnp
from jax import lax
from jax.experimental import pallas as pl
from jax.experimental.pallas import tpu as pltpu
from jax.sharding import PartitionSpec as P

F32 = jnp.float32
BF16 = jnp.bfloat16
HALF_AZ = 5
HALF_RG = 11
LANES = 128
MESH = pl.DeviceIdType.MESH
OWN, ABOVE, BELOW = 0, 9, 15
PLANES = 21


def pack_tile(tiles, snd, groups, rows, dates):
    lane = lax.broadcasted_iota(jnp.int32, (8, LANES), 1)

    per = tiles.shape[0] // groups

    def plane(l, c, r):
        return snd[l // per, 1 + r, c * per + l % per]

    for l in range(tiles.shape[0]):
        for c in range(2):
            block = tiles[l, c * dates * rows:(c * dates + 8) * rows].reshape(8, rows, LANES)
            block = jnp.swapaxes(block, 0, 1)
            for r in range(rows):
                snd[l // per, 1 + r, c * per + l % per] = block[r]
    for d in range(groups):
        for c in range(2):
            for t in range(2):
                tail = jnp.zeros((8, LANES), F32)
                for q in range(4):
                    at = 32 * q
                    if d > 0:
                        left = pltpu.roll(plane(d * per - 1, c, 4 * t + q), (at + HALF_RG) % LANES, 1)
                        tail = jnp.where((lane >= at) & (lane < at + HALF_RG), left, tail)
                    if d < groups - 1:
                        right = plane((d + 1) * per, c, 4 * t + q)
                        right = pltpu.roll(right, at + HALF_RG, 1)
                        tail = jnp.where((lane >= at + HALF_RG) & (lane < at + 2 * HALF_RG), right, tail)
                snd[d, 0, 2 * c + t] = tail
                snd[d, 9, 2 * c + t] = tail


def exchange(groups, spaces, rows, dates, x_ref, rcv, tiles, snd, in_sem, self_sem, send_sem, recv_sem):
    g = lax.axis_index("date")
    s = lax.axis_index("space")
    loads = []
    for l in range(tiles.shape[0]):
        n = x_ref.shape[0]
        loads.append(
            pltpu.make_async_copy(
                x_ref.at[:, pl.ds(l * LANES, LANES)], tiles.at[l, pl.ds(0, n)], in_sem.at[l]
            )
        )
        loads[-1].start()
        tiles[l, pl.ds(n, 16)] = jnp.zeros((16, LANES), F32)

    up = lax.rem(s + spaces - 1, spaces)
    down = lax.rem(s + 1, spaces)
    barrier = pltpu.get_barrier_semaphore()

    def greet(d, to):
        pl.semaphore_signal(barrier, inc=1, device_id={"date": d, "space": to}, device_id_type=MESH)

    for off in range(groups):
        d = lax.rem(g + off, groups)
        greet(d, up)
        greet(d, down)
        if off:
            greet(d, s)
    for copy in loads:
        copy.wait()
    pack_tile(tiles, snd, groups, rows, dates)
    pl.semaphore_wait(barrier, 3 * groups - 1)

    def copy_of(kind, off, to, first, count, at, source):
        d = lax.rem(g + off, groups)
        return pltpu.make_async_remote_copy(
            src_ref=snd.at[d, pl.ds(first, count)],
            dst_ref=rcv.at[source, pl.ds(at, count)],
            send_sem=send_sem.at[kind * groups + off],
            recv_sem=recv_sem.at[kind * groups + off],
            device_id={"date": d, "space": to},
            device_id_type=MESH,
        )

    sent = []
    for off in (2, 3, 1, 0):
        sent.append((0, off, up, 0, 6, BELOW))
        sent.append((1, off, down, 4, 6, ABOVE))
        if off:
            sent.append((2, off, s, 0, 9, OWN))
    for args in sent:
        copy_of(*args, g).start()
    keep = pltpu.make_async_copy(snd.at[g, pl.ds(0, 9)], rcv.at[g, pl.ds(OWN, 9)], self_sem)
    keep.start()
    keep.wait()
    for args in sent:
        copy_of(*args, lax.rem(g + groups - args[1], groups)).wait_recv()
    for args in sent:
        copy_of(*args, g).wait_send()

    @pl.when(s == 0)
    def _():
        rcv[:, ABOVE:ABOVE + 6] = jnp.zeros((groups, 6) + rcv.shape[2:], F32)

    @pl.when(s == spaces - 1)
    def _():
        rcv[:, BELOW:BELOW + 6] = jnp.zeros((groups, 6) + rcv.shape[2:], F32)


def source_of(row):
    if row < HALF_AZ:
        own = row + 3
        return ABOVE + row, ABOVE + 5, own // 4, own % 4
    if row < HALF_AZ + 8:
        own = row - HALF_AZ
        return OWN + 1 + own, OWN, own // 4, own % 4
    own = row - HALF_AZ - 8
    return BELOW + 1 + own, BELOW, own // 4, own % 4


def window(p):
    suffix = [None] * 8
    suffix[7] = (p[7] + p[8]) + (p[9] + p[10])
    for r in range(6, -1, -1):
        suffix[r] = suffix[r + 1] + p[r]
    out = [suffix[0]]
    prefix = p[11]
    for r in range(1, 8):
        out.append(suffix[r] + prefix)
        if r < 7:
            prefix = prefix + p[11 + r]
    return out


def split(v):
    high = v.astype(BF16).astype(F32)
    return high, v - high


def unpack(rcv, main, tail, wide, groups, dates):
    lane = lax.broadcasted_iota(jnp.int32, (24, LANES), 1)
    for c in range(2):
        for row in range(18):
            plane = source_of(row)[0]
            for l in range(2):
                for h in range(2 * groups):
                    main[c, row, l, pl.ds(dates * h, dates)] = rcv[h % groups, plane, 2 * c + l, 0:dates]
        for n, plane in enumerate((OWN, ABOVE + 5, BELOW)):
            for t in range(2):
                for h in range(2 * groups):
                    wide[c, n, t, pl.ds(dates * h, dates)] = rcv[h % groups, plane, 2 * c + t, 0:dates]
        for row in range(18):
            _, plane, t, q = source_of(row)
            n = (OWN, ABOVE + 5, BELOW).index(plane)
            packed = None
            for b in range(4):
                part = wide[c, n, t, pl.ds(8 * b, 24)]
                if b != q:
                    part = pltpu.roll(part, (32 * (b - q)) % LANES, 1)
                packed = part if packed is None else jnp.where(lane >= 32 * b, part, packed)
            tail[c, row] = packed


def fill_lhs(shift, main, tail, lhs, power_only):
    comps = 1 if power_only else 2
    for l in range(2):
        for b in range(2):
            first, second = [], []
            for row in range(18):
                a = main[0, row, l, pl.ds(16 * b, 16)]
                e = main[1, row, l, pl.ds(16 * b, 16)]
                if power_only:
                    first.append(a * a + e * e)
                else:
                    ao = main[0, row, l, pl.ds(16 * b + shift, 16)]
                    eo = main[1, row, l, pl.ds(16 * b + shift, 16)]
                    first.append(a * ao + e * eo)
                    second.append(e * ao - a * eo)
            for c, planes in enumerate((first, second)[:comps]):
                for r, v in enumerate(window(planes)):
                    high, low = split(v)
                    at = pl.ds(256 * c + 32 * r + 16 * b, 16)
                    lhs[at, LANES * l:LANES * (l + 1)] = high.astype(BF16)
                    lhs[at, LANES * (2 + l):LANES * (3 + l)] = low.astype(BF16)
    first, second = [], []
    for row in range(18):
        a = tail[0, row, 0:8]
        e = tail[1, row, 0:8]
        if power_only:
            first.append(a * a + e * e)
        else:
            ao = tail[0, row, pl.ds(shift, 8)]
            eo = tail[1, row, pl.ds(shift, 8)]
            first.append(a * ao + e * eo)
            second.append(e * ao - a * eo)
    block = lax.broadcasted_iota(jnp.int32, (8, LANES), 1) // 32
    for c, planes in enumerate((first, second)[:comps]):
        for r, v in enumerate(window(planes)):
            for n, part in enumerate(split(v)):
                for b in range(2):
                    both = jnp.concatenate(
                        [jnp.where(block == 2 * b + h, part, 0.0) for h in range(2)], axis=0
                    )
                    lhs[pl.ds(256 * c + 32 * r + 16 * b, 16), LANES * (4 + n):LANES * (5 + n)] = both.astype(BF16)


def pairs(groups, dates, rcv, out, main, tail, wide, lhs, res, inv, band):
    k = pl.program_id(0)
    total = groups * dates

    @pl.when(k == 0)
    def _():
        i = lax.broadcasted_iota(jnp.int32, (256, 256), 0)
        o = lax.broadcasted_iota(jnp.int32, (256, 256), 1)
        centre = jnp.where((i >= o - HALF_RG) & (i <= o + HALF_RG), 1.0, 0.0).astype(BF16)
        it = lax.broadcasted_iota(jnp.int32, (128, 256), 0) % 32
        ot = lax.broadcasted_iota(jnp.int32, (128, 256), 1)
        col = jnp.where(it < HALF_RG, it - HALF_RG, 256 + it - HALF_RG)
        edge = jnp.where(
            (it < 2 * HALF_RG) & (col >= ot - HALF_RG) & (col <= ot + HALF_RG), 1.0, 0.0
        ).astype(BF16)
        band[0:256] = centre
        band[256:512] = centre
        band[512:640] = edge
        band[640:768] = edge
        unpack(rcv, main, tail, wide, groups, dates)
        fill_lhs(0, main, tail, lhs, True)
        power = jnp.dot(lhs[0:256], band[...], preferred_element_type=F32)
        for l in range(2):
            res[0, l, 0:256] = lax.rsqrt(power[:, LANES * l:LANES * (l + 1)])
        for d in range(total):
            for l in range(2):
                inv[d, :, LANES * l:LANES * (l + 1)] = res[0, l, pl.ds(d, 8, stride=32), :]

    fill_lhs(k + 1, main, tail, lhs, False)
    both = jnp.dot(lhs[...], band[...], preferred_element_type=F32)
    for c in range(2):
        for l in range(2):
            res[c, l, 0:256] = both[256 * c:256 * (c + 1), LANES * l:LANES * (l + 1)]
    for d in range(total):
        other = lax.rem(d + k + 1, total)
        for l in range(2):
            cols = slice(LANES * l, LANES * (l + 1))
            re = res[0, l, pl.ds(d, 8, stride=32), :]
            im = res[1, l, pl.ds(d, 8, stride=32), :]
            out[0, d, :, cols] = jnp.sqrt(re * re + im * im) * (inv[d, :, cols] * inv[other, :, cols])


def body(groups, spaces, stack):
    _, dates, rows, cols = stack.shape
    n_tiles = cols // LANES
    lags = groups * dates // 2
    flat = stack.reshape(2 * dates * rows, cols)
    rcv = pl.pallas_call(
        functools.partial(exchange, groups, spaces, rows, dates),
        out_shape=jax.ShapeDtypeStruct((groups, PLANES, 4, 8, LANES), F32),
        in_specs=[pl.BlockSpec(memory_space=pl.ANY)],
        out_specs=pl.BlockSpec(memory_space=pltpu.VMEM),
        scratch_shapes=[
            pltpu.VMEM((n_tiles, 2 * dates * rows + 16, LANES), F32),
            pltpu.VMEM((groups, 10, 4, 8, LANES), F32),
            pltpu.SemaphoreType.DMA((n_tiles,)),
            pltpu.SemaphoreType.DMA,
            pltpu.SemaphoreType.DMA((3 * groups,)),
            pltpu.SemaphoreType.DMA((3 * groups,)),
        ],
        compiler_params=pltpu.CompilerParams(
            collective_id=0, has_side_effects=True, vmem_limit_bytes=24 << 20
        ),
        name="exchange",
    )(flat)
    width = cols // groups
    return pl.pallas_call(
        functools.partial(pairs, groups, dates),
        grid=(lags,),
        out_shape=jax.ShapeDtypeStruct((lags, groups * dates, rows, width), F32),
        in_specs=[pl.BlockSpec(rcv.shape, lambda k: (0,) * 5)],
        out_specs=pl.BlockSpec((1, groups * dates, rows, width), lambda k: (k, 0, 0, 0)),
        scratch_shapes=[
            pltpu.VMEM((2, 18, 2, 56, LANES), F32),
            pltpu.VMEM((2, 18, 24, LANES), F32),
            pltpu.VMEM((2, 3, 2, 56, LANES), F32),
            pltpu.VMEM((512, 6 * LANES), BF16),
            pltpu.VMEM((2, 2, 288, LANES), F32),
            pltpu.VMEM((groups * dates, rows, width), F32),
            pltpu.VMEM((6 * LANES, 256), BF16),
        ],
        compiler_params=pltpu.CompilerParams(vmem_limit_bytes=32 << 20),
        name="pairs",
    )(rcv)


def solution(mesh):
    groups, spaces = mesh.shape["date"], mesh.shape["space"]
    return jax.shard_map(
        functools.partial(body, groups, spaces),
        mesh=mesh,
        in_specs=(P(None, "date", "space", None),),
        out_specs=P(None, None, "space", "date"),
        check_vma=False,
    )
```

time: 219 us -> 41.8 us (0.19)
  the two profiles are of different devices: /device:TPU:25 before, /device:TPU:0 now
where the time goes in v1:
time: 41.8 us; the launch traced here: 41.7 us
  Pallas kernels  40.6 us (97%)
  local copies, waits for them, and re-layouts  1.02 us (2%)
    pallas_call x1, Pallas kernels, body(): pl.pallas_call(functools.partial(exchange, groups, spaces, rows, dates),...  23.8 us
    pallas_call x1, Pallas kernels, body(): pl.pallas_call(functools.partial(pairs, groups, dates), grid=(lags,), out...  16.9 us
    unnamed x2, local copies, waits for them, and re-layouts  1.02 us

profile of v1, /device:TPU:0, one launch (start us, length us, event | category | flops | bytes accessed | tf_op | source)
XLA Modules:
  0.0 41.7 jit_solution(10724639608852708655)
XLA Ops:
  0.0 0.0 copy-start
  0.0 1.0 %copy-done = f32[2,7,8,1024]{3,2,1,0:T(8,128)S(1)} copy-done((f32[2,7,8,1024]{3,2,1,0:T(8,128)S(1)}, f32[2,7,8,1024]{3,2,1,0:T(8,128)}, u32[]{:S(2)}) %copy-start) | copy-done | bytes 458776
  1.0 23.8 %exchange.1.rcv = f32[4,21,4,8,128]{4,3,2,1,0:T(8,128)S(1)} custom-call(f32[112,1024]{1,0:T(8,128)S(1)} %bitcast.1), custom_call_target="tpu_custom_call" | custom-call | tf_op jit(solution)/shard_map/exchange/pallas_call | solution.py:263
  24.8 16.9 %pairs.1 = f32[14,28,8,256]{3,2,1,0:T(8,128)} custom-call(f32[4,21,4,8,128]{4,3,2,1,0:T(8,128)S(1)} %exchange.1.rcv), custom_call_target="tpu_custom_call" | custom-call | tf_op jit(solution)/shard_map/pairs/pallas_call | solution.py:282
Async XLA Ops:
  0.0 1.0 %copy-start = (f32[2,7,8,1024]{3,2,1,0:T(8,128)S(1)}, f32[2,7,8,1024]{3,2,1,0:T(8,128)}, u32[]{:S(2)}) copy-start(f32[2,7,8,1024]{3,2,1,0:T(8,128)} %param.1) | copy-start | bytes 1376260

commit v2 on v1

--- a/solution.py
+++ b/solution.py
@@ -213,7 +213,7 @@
                     lhs[pl.ds(256 * c + 32 * r + 16 * b, 16), LANES * (4 + n):LANES * (5 + n)] = both.astype(BF16)
 
 
-def pairs(groups, dates, rcv, out, main, tail, wide, lhs, res, inv, band):
+def pairs(groups, dates, rcv, out, main, tail, wide, lhs, lhs_b, res, res_b, inv, band):
     k = pl.program_id(0)
     total = groups * dates
 
@@ -241,18 +241,20 @@
             for l in range(2):
                 inv[d, :, LANES * l:LANES * (l + 1)] = res[0, l, pl.ds(d, 8, stride=32), :]
 
-    fill_lhs(k + 1, main, tail, lhs, False)
-    both = jnp.dot(lhs[...], band[...], preferred_element_type=F32)
-    for c in range(2):
-        for l in range(2):
-            res[c, l, 0:256] = both[256 * c:256 * (c + 1), LANES * l:LANES * (l + 1)]
-    for d in range(total):
-        other = lax.rem(d + k + 1, total)
-        for l in range(2):
-            cols = slice(LANES * l, LANES * (l + 1))
-            re = res[0, l, pl.ds(d, 8, stride=32), :]
-            im = res[1, l, pl.ds(d, 8, stride=32), :]
-            out[0, d, :, cols] = jnp.sqrt(re * re + im * im) * (inv[d, :, cols] * inv[other, :, cols])
+    for n, (left, sums) in enumerate(((lhs, res), (lhs_b, res_b))):
+        fill_lhs(2 * k + n + 1, main, tail, left, False)
+        both = jnp.dot(left[...], band[...], preferred_element_type=F32)
+        for c in range(2):
+            for l in range(2):
+                sums[c, l, 0:256] = both[256 * c:256 * (c + 1), LANES * l:LANES * (l + 1)]
+    for n, sums in enumerate((res, res_b)):
+        for d in range(total):
+            other = lax.rem(d + 2 * k + n + 1, total)
+            for l in range(2):
+                cols = slice(LANES * l, LANES * (l + 1))
+                re = sums[0, l, pl.ds(d, 8, stride=32), :]
+                im = sums[1, l, pl.ds(d, 8, stride=32), :]
+                out[n, d, :, cols] = jnp.sqrt(re * re + im * im) * (inv[d, :, cols] * inv[other, :, cols])
 
 
 def body(groups, spaces, stack):
@@ -281,15 +283,17 @@
     width = cols // groups
     return pl.pallas_call(
         functools.partial(pairs, groups, dates),
-        grid=(lags,),
+        grid=(lags // 2,),
         out_shape=jax.ShapeDtypeStruct((lags, groups * dates, rows, width), F32),
         in_specs=[pl.BlockSpec(rcv.shape, lambda k: (0,) * 5)],
-        out_specs=pl.BlockSpec((1, groups * dates, rows, width), lambda k: (k, 0, 0, 0)),
+        out_specs=pl.BlockSpec((2, groups * dates, rows, width), lambda k: (k, 0, 0, 0)),
         scratch_shapes=[
             pltpu.VMEM((2, 18, 2, 56, LANES), F32),
             pltpu.VMEM((2, 18, 24, LANES), F32),
             pltpu.VMEM((2, 3, 2, 56, LANES), F32),
             pltpu.VMEM((512, 6 * LANES), BF16),
+            pltpu.VMEM((512, 6 * LANES), BF16),
+            pltpu.VMEM((2, 2, 288, LANES), F32),
             pltpu.VMEM((2, 2, 288, LANES), F32),
             pltpu.VMEM((groups * dates, rows, width), F32),
             pltpu.VMEM((6 * LANES, 256), BF16),

time: 41.8 us -> 40.1 us (0.959)
  Pallas kernels: 40.6 us -> 39 us
    pallas_call x1, Pallas kernels: 16.9 us -> 15.2 us  [body(): pl.pallas_call(functools.partial(pairs, groups, dates), grid=(lags // 2,)...]
where the time goes in v2:
time: 40.1 us; the launch traced here: 40 us
  Pallas kernels  39 us (97%)
  local copies, waits for them, and re-layouts  1.02 us (3%)
    pallas_call x1, Pallas kernels, body(): pl.pallas_call(functools.partial(exchange, groups, spaces, rows, dates),...  23.8 us
    pallas_call x1, Pallas kernels, body(): pl.pallas_call(functools.partial(pairs, groups, dates), grid=(lags // 2,)...  15.2 us
    unnamed x2, local copies, waits for them, and re-layouts  1.02 us

profile of v2, /device:TPU:0, one launch (start us, length us, event | category | flops | bytes accessed | tf_op | source)
XLA Modules:
  0.0 40.0 jit_solution(13742886496020124189)
XLA Ops:
  0.0 0.0 copy-start
  0.0 1.0 %copy-done = f32[2,7,8,1024]{3,2,1,0:T(8,128)S(1)} copy-done((f32[2,7,8,1024]{3,2,1,0:T(8,128)S(1)}, f32[2,7,8,1024]{3,2,1,0:T(8,128)}, u32[]{:S(2)}) %copy-start) | copy-done | bytes 458776
  1.0 23.8 %exchange.1.rcv = f32[4,21,4,8,128]{4,3,2,1,0:T(8,128)S(1)} custom-call(f32[112,1024]{1,0:T(8,128)S(1)} %bitcast.1), custom_call_target="tpu_custom_call" | custom-call | tf_op jit(solution)/shard_map/exchange/pallas_call | solution.py:265
  24.8 15.2 %pairs.1 = f32[14,28,8,256]{3,2,1,0:T(8,128)} custom-call(f32[4,21,4,8,128]{4,3,2,1,0:T(8,128)S(1)} %exchange.1.rcv), custom_call_target="tpu_custom_call" | custom-call | tf_op jit(solution)/shard_map/pairs/pallas_call | solution.py:284
Async XLA Ops:
  0.0 1.0 %copy-start = (f32[2,7,8,1024]{3,2,1,0:T(8,128)S(1)}, f32[2,7,8,1024]{3,2,1,0:T(8,128)}, u32[]{:S(2)}) copy-start(f32[2,7,8,1024]{3,2,1,0:T(8,128)} %param.1) | copy-start | bytes 1376260

commit v3 on v2

--- a/solution.py
+++ b/solution.py
@@ -97,15 +97,31 @@
         sent.append((1, off, down, 4, 6, ABOVE))
         if off:
             sent.append((2, off, s, 0, 9, OWN))
-    for args in sent:
-        copy_of(*args, g).start()
+    def each(use):
+        for kind, there in ((0, s > 0), (1, s < spaces - 1)):
+            @pl.when(there)
+            def _():
+                for args in sent:
+                    if args[0] == kind:
+                        use(kind, args)
+        for args in sent:
+            if args[0] == 2:
+                use(2, args)
+
+    each(lambda kind, args: copy_of(*args, g).start())
     keep = pltpu.make_async_copy(snd.at[g, pl.ds(0, 9)], rcv.at[g, pl.ds(OWN, 9)], self_sem)
     keep.start()
     keep.wait()
+    for kind, there in ((0, s < spaces - 1), (1, s > 0)):
+        @pl.when(there)
+        def _():
+            for args in sent:
+                if args[0] == kind:
+                    copy_of(*args, lax.rem(g + groups - args[1], groups)).wait_recv()
     for args in sent:
-        copy_of(*args, lax.rem(g + groups - args[1], groups)).wait_recv()
-    for args in sent:
-        copy_of(*args, g).wait_send()
+        if args[0] == 2:
+            copy_of(*args, lax.rem(g + groups - args[1], groups)).wait_recv()
+    each(lambda kind, args: copy_of(*args, g).wait_send())
 
     @pl.when(s == 0)
     def _():

time: 40.1 us -> 39.2 us (0.978)
  Pallas kernels: 39 us -> 38 us
    pallas_call x1, Pallas kernels: 23.8 us -> 22.9 us  [body(): pl.pallas_call(functools.partial(exchange, groups, spaces, rows, dates),...]
where the time goes in v3:
time: 39.2 us; the launch traced here: 39.1 us
  Pallas kernels  38 us (97%)
  local copies, waits for them, and re-layouts  1.02 us (3%)
    pallas_call x1, Pallas kernels, body(): pl.pallas_call(functools.partial(exchange, groups, spaces, rows, dates),...  22.9 us
    pallas_call x1, Pallas kernels, body(): pl.pallas_call(functools.partial(pairs, groups, dates), grid=(lags // 2,)...  15.2 us
    unnamed x2, local copies, waits for them, and re-layouts  1.02 us

profile of v3, /device:TPU:0, one launch (start us, length us, event | category | flops | bytes accessed | tf_op | source)
XLA Modules:
  0.0 39.1 jit_solution(17197126375611852681)
XLA Ops:
  0.0 0.0 copy-start
  0.0 1.0 %copy-done = f32[2,7,8,1024]{3,2,1,0:T(8,128)S(1)} copy-done((f32[2,7,8,1024]{3,2,1,0:T(8,128)S(1)}, f32[2,7,8,1024]{3,2,1,0:T(8,128)}, u32[]{:S(2)}) %copy-start) | copy-done | bytes 458776
  1.0 22.9 %exchange.1.rcv = f32[4,21,4,8,128]{4,3,2,1,0:T(8,128)S(1)} custom-call(f32[112,1024]{1,0:T(8,128)S(1)} %bitcast.1), custom_call_target="tpu_custom_call" | custom-call | tf_op jit(solution)/shard_map/exchange/pallas_call | solution.py:281
  23.9 15.2 %pairs.1 = f32[14,28,8,256]{3,2,1,0:T(8,128)} custom-call(f32[4,21,4,8,128]{4,3,2,1,0:T(8,128)S(1)} %exchange.1.rcv), custom_call_target="tpu_custom_call" | custom-call | tf_op jit(solution)/shard_map/pairs/pallas_call | solution.py:300
Async XLA Ops:
  0.0 1.0 %copy-start = (f32[2,7,8,1024]{3,2,1,0:T(8,128)S(1)}, f32[2,7,8,1024]{3,2,1,0:T(8,128)}, u32[]{:S(2)}) copy-start(f32[2,7,8,1024]{3,2,1,0:T(8,128)} %param.1) | copy-start | bytes 1376260

commit v4 on v3

--- a/solution.py
+++ b/solution.py
@@ -281,7 +281,7 @@
     rcv = pl.pallas_call(
         functools.partial(exchange, groups, spaces, rows, dates),
         out_shape=jax.ShapeDtypeStruct((groups, PLANES, 4, 8, LANES), F32),
-        in_specs=[pl.BlockSpec(memory_space=pl.ANY)],
+        in_specs=[pl.BlockSpec(memory_space=pltpu.HBM)],
         out_specs=pl.BlockSpec(memory_space=pltpu.VMEM),
         scratch_shapes=[
             pltpu.VMEM((n_tiles, 2 * dates * rows + 16, LANES), F32),

time: 39.2 us -> 39.2 us (level)
  no operation moved by 1% of the time
where the time goes in v4:
time: 39.2 us; the launch traced here: 39.1 us
  Pallas kernels  38 us (97%)
  local copies, waits for them, and re-layouts  1.02 us (3%)
    pallas_call x1, Pallas kernels, body(): pl.pallas_call(functools.partial(exchange, groups, spaces, rows, dates),...  22.9 us
    pallas_call x1, Pallas kernels, body(): pl.pallas_call(functools.partial(pairs, groups, dates), grid=(lags // 2,)...  15.2 us
    unnamed x2, local copies, waits for them, and re-layouts  1.02 us

profile of v4, /device:TPU:0, one launch (start us, length us, event | category | flops | bytes accessed | tf_op | source)
XLA Modules:
  0.0 39.1 jit_solution(17197126375611852681)
XLA Ops:
  0.0 0.0 copy-start
  0.0 1.0 %copy-done = f32[2,7,8,1024]{3,2,1,0:T(8,128)S(1)} copy-done((f32[2,7,8,1024]{3,2,1,0:T(8,128)S(1)}, f32[2,7,8,1024]{3,2,1,0:T(8,128)}, u32[]{:S(2)}) %copy-start) | copy-done | bytes 458776
  1.0 22.9 %exchange.1.rcv = f32[4,21,4,8,128]{4,3,2,1,0:T(8,128)S(1)} custom-call(f32[112,1024]{1,0:T(8,128)S(1)} %bitcast.1), custom_call_target="tpu_custom_call" | custom-call | tf_op jit(solution)/shard_map/exchange/pallas_call | solution.py:281
  23.9 15.2 %pairs.1 = f32[14,28,8,256]{3,2,1,0:T(8,128)} custom-call(f32[4,21,4,8,128]{4,3,2,1,0:T(8,128)S(1)} %exchange.1.rcv), custom_call_target="tpu_custom_call" | custom-call | tf_op jit(solution)/shard_map/pairs/pallas_call | solution.py:300
Async XLA Ops:
  0.0 1.0 %copy-start = (f32[2,7,8,1024]{3,2,1,0:T(8,128)S(1)}, f32[2,7,8,1024]{3,2,1,0:T(8,128)}, u32[]{:S(2)}) copy-start(f32[2,7,8,1024]{3,2,1,0:T(8,128)} %param.1) | copy-start | bytes 1376260
